TPU v7x, 32 devices: a whole 2x2x4 slice. The times are simulated.
32 devices in a mesh: ublk: 8 (over z, x), salt: 4 (over y, core).
Axes of the slice: x: 2, y: 2, z: 4, core: 2. Of those that a mesh axis runs over, the one named last changes fastest.
Arguments:
- user_factors: bfloat16 [8, 4096, 256], P('ublk', 'salt')
- tile_users: int32 [8, 4, 4096], P('ublk', 'salt'), may hold values from 0 to 4095
- tile_items: int32 [8, 4, 4096], P('ublk', 'salt'), may hold values from 0 to 255
- tile_weight: float32 [8, 4, 4096], P('ublk', 'salt'), may hold values from 0.5 to 8
- live_count: int32 [8, 4], P('ublk', 'salt'), may hold values from 2048 to 4096, as said below
Outputs:
- item_factors: float32 [4, 256, 256], P('salt', 'ublk')
- residual: float32 [4, 256, 256], P('salt', 'ublk')
Inputs may be any that keep to these rules, and one draw needn't show every extreme that they name: Every entry of live_count is at least 2048 and at most 4096; some tile is full.
All inputs are finite; a program needn't handle non-finite values.
Results may differ from a plain program's by a relative error of at most 0.0022.
Values may be sent and summed in bfloat16 or wider, within the bound.
No kernel may reach another device: no remote copies, remote signals or barrier semaphores. Data moves between devices by JAX's collectives and lax.ppermute only.
A program may use at most 64 MiB of HBM per device.

v0:
```python
import jax
import jax.numpy as jnp
from jax import lax
from jax.sharding import PartitionSpec as P

ITERS = 8
ITEM_DEV = 32


REG = 1.0
EPS = 1e-06


def conjugate(rhs, image_of):
    solution = jnp.zeros_like(rhs)
    resid = rhs
    direction = rhs
    norm_now = jnp.sum(resid * resid, axis=1)
    for step in range(ITERS):
        image = image_of(direction)
        alpha = norm_now / (jnp.sum(direction * image, axis=1) + EPS)
        solution = solution + alpha[:, None] * direction
        resid = resid - alpha[:, None] * image
        norm_next = jnp.sum(resid * resid, axis=1)
        direction = resid + (norm_next / (norm_now + EPS))[:, None] * direction
        norm_now = norm_next
    return (solution, resid)


def body(user_factors, tile_users, tile_items, tile_weight, live_count):
    shard = user_factors[0]
    block = lax.all_gather(shard, "salt", axis=0, tiled=True)
    contract = (((0,), (0,)), ((), ()))
    own_gram = lax.dot_general(block, block, contract, preferred_element_type=jnp.float32)
    gram = lax.psum(own_gram, "ublk")
    users = tile_users[0, 0]
    items = tile_items[0, 0]
    raw = tile_weight[0, 0]
    live = jnp.arange(users.shape[0], dtype=jnp.int32) < live_count[0, 0]
    weight = jnp.where(live, raw, jnp.zeros_like(raw))
    confid = jnp.where(live, 1.0 + raw, jnp.zeros_like(raw))
    rows = jnp.take(block, users, axis=0).astype(jnp.float32)
    column_items = ITEM_DEV * lax.axis_size("ublk")
    rhs_terms = jax.ops.segment_sum(confid[:, None] * rows, items, num_segments=column_items)

    def local_terms(whole_dir):
        along = jnp.sum(rows * whole_dir[items], axis=1) * weight
        return jax.ops.segment_sum(along[:, None] * rows, items, num_segments=column_items)

    def finish(summed, direction):
        return summed + jnp.dot(direction, gram, precision=lax.Precision.HIGHEST) + REG * direction

    rhs = lax.psum(rhs_terms, "ublk")

    def image_every(direction):
        summed = lax.psum(local_terms(direction), "ublk")
        return finish(summed, direction)

    solution_all, resid_all = conjugate(rhs, image_every)
    start = lax.axis_index("ublk") * ITEM_DEV
    solution = lax.dynamic_slice_in_dim(solution_all, start, ITEM_DEV, 0)
    resid = lax.dynamic_slice_in_dim(resid_all, start, ITEM_DEV, 0)
    return (solution[None], resid[None])


def solution(mesh):
    return jax.shard_map(
        body,
        mesh=mesh,
        in_specs=(
            P("ublk", "salt", None),
            P("ublk", "salt", None),
            P("ublk", "salt", None),
            P("ublk", "salt", None),
            P("ublk", "salt"),
        ),
        out_specs=(P("salt", "ublk", None), P("salt", "ublk", None)),
        check_vma=False,
    )
```

profile of v0, /device:TPU:23, one launch (start us, length us, event | category | flops | bytes accessed | tf_op | source)
XLA Modules:
  0.0 1101.7 jit_solution(967627680595604075)
XLA Ops:
  7.2 0.7 all-gather.3.cloned.1.call-update
  8.6 0.7 compare_and_fusion
  9.3 0.7 compare_select_fusion.1
  10.1 0.7 compare_select_fusion
  10.8 0.7 add_select_fusion
  11.5 21.1 %all-gather.3.cloned.1.call-done = bf16[1,4096,256]{2,1,0:T(8,128)(2,1)} async-done(((bf16[1,1024,256]{2,1,0:T(8,128)(2,1)}), bf16[1,4096,256]{2,1,0:T(8,128)(2,1)}) %all-gather.3.cloned.1.call-update) | async-done | bytes 2097168 | tf_op jit(solution)/shard_map/all_gather | solution.py:32
  32.7 14.9 %gather_fusion = bf16[4096,256]{1,0:T(8,128)(2,1)S(1)} fusion(bf16[4096,256]{1,0:T(8,128)(2,1)} %bitcast.42, s32[4096]{0:T(1024)S(1)} %broadcast_clamp_fusion.1), kind=kCustom, calls=%fused_computation | custom fusion | bytes 4210688 | tf_op jit(solution)/shard_map/jit(_take)/gather | solution.py:42
  47.5 26.1 %scatter_custom_fusion = f32[256,256]{1,0:T(8,128)} fusion(s32[4096]{0:T(1024)} %bitcast.55, f32[4096]{0:T(1024)S(1)} %add_select_fusion, f32[]{:T(128)} %constant.11.clone.1, bf16[4096,256]{1,0:T(8,128)(2,1)S(1)} %gather_fusion, pred[4096]{0:T(1024)(128)(4,1)S(1)} %compare_and_fusion), kind=kCustom, calls=%fused_computation.35 | custom fusion | flops 4194304 | bytes 2380288 | tf_op jit(solution)/shard_map/scatter-add | solution.py:44
  73.7 3.7 fusion.59
  77.4 64.8 %all-reduce.11.cloned.1.call-done = f32[256,256]{1,0:T(8,128)} async-done(((f32[256,256]{1,0:T(8,128)}), f32[256,256]{1,0:T(8,128)}) %all-reduce.11.cloned.1.call-update) | async-done | bytes 262160 | tf_op jit(solution)/shard_map/psum | solution.py:53
  142.2 17.0 %gather_fusion.1 = f32[4096,256]{1,0:T(8,128)} fusion(f32[256,256]{1,0:T(8,128)} %all-reduce.11.cloned.1.call-done, s32[4096]{0:T(1024)S(1)} %broadcast_clamp_fusion), kind=kCustom, calls=%fused_computation.1 | custom fusion | bytes 8404992 | tf_op jit(solution)/shard_map/gather | solution.py:47
  159.2 3.0 fusion.1
  162.2 26.1 %scatter_custom_fusion.1 = f32[256,256]{1,0:T(8,128)} fusion(s32[4096]{0:T(1024)} %bitcast.56, f32[4096]{0:T(1024)S(1)} %fusion.58, f32[]{:T(128)} %constant.11.clone.1, bf16[4096,256]{1,0:T(8,128)(2,1)S(1)} %gather_fusion, pred[4096]{0:T(1024)(128)(4,1)S(1)} %compare_and_fusion), kind=kCustom, calls=%fused_computation.37 | custom fusion | flops 4194304 | bytes 2380288 | tf_op jit(solution)/shard_map/scatter-add | solution.py:48
  188.4 72.2 %all-reduce.27.cloned.1.call-done = (f32[256,256]{1,0:T(8,128)}, f32[256,256]{1,0:T(8,128)}) async-done(((f32[256,256]{1,0:T(8,128)}, f32[256,256]{1,0:T(8,128)}), (f32[256,256]{1,0:T(8,128)}, f32[256,256]{1,0:T(8,128)})) %all-reduce.27.cloned.1.call-update) | async-done | bytes 524304 | tf_op jit(solution)/shard_map/psum | solution.py:56
  260.6 1.5 multiply_reduce_fusion.14
  262.1 0.2 multiply_reduce_fusion.13
  262.3 0.1 multiply_add_fusion.7
  262.5 16.1 %gather_fusion.2 = f32[4096,256]{1,0:T(8,128)} fusion(f32[256,256]{1,0:T(8,128)S(1)} %multiply_add_fusion.7, s32[4096]{0:T(1024)S(1)} %broadcast_clamp_fusion), kind=kCustom, calls=%fused_computation.2 | custom fusion | bytes 8404992 | tf_op jit(solution)/shard_map/gather | solution.py:47
  278.6 3.0 fusion.3
  281.6 26.1 %scatter_custom_fusion.2 = f32[256,256]{1,0:T(8,128)} fusion(s32[4096]{0:T(1024)} %bitcast.57, f32[4096]{0:T(1024)S(1)} %fusion.57, f32[]{:T(128)} %constant.11.clone.1, bf16[4096,256]{1,0:T(8,128)(2,1)S(1)} %gather_fusion, pred[4096]{0:T(1024)(128)(4,1)S(1)} %compare_and_fusion), kind=kCustom, calls=%fused_computation.39 | custom fusion | flops 4194304 | bytes 2380288 | tf_op jit(solution)/shard_map/scatter-add | solution.py:48
  307.7 0.3 all-reduce.15.cloned.1.call-start
  308.0 69.3 %all-reduce.13.cloned.1.call-done = f32[256,256]{1,0:T(8,128)} async-done(((f32[256,256]{1,0:T(8,128)}), f32[256,256]{1,0:T(8,128)}) %all-reduce.13.cloned.1.call-update) | async-done | bytes 262160 | tf_op jit(solution)/shard_map/psum | solution.py:56
  377.3 1.4 multiply_reduce_fusion.12
  378.7 0.9 multiply_reduce_fusion.11
  379.6 0.1 multiply_add_fusion.5
  379.7 16.1 %gather_fusion.3 = f32[4096,256]{1,0:T(8,128)} fusion(f32[256,256]{1,0:T(8,128)S(1)} %multiply_add_fusion.5, s32[4096]{0:T(1024)S(1)} %broadcast_clamp_fusion), kind=kCustom, calls=%fused_computation.3 | custom fusion | bytes 8404992 | tf_op jit(solution)/shard_map/gather | solution.py:47
  395.8 2.9 fusion.5
  398.7 26.1 %scatter_custom_fusion.3 = f32[256,256]{1,0:T(8,128)} fusion(s32[4096]{0:T(1024)} %bitcast.58, f32[4096]{0:T(1024)S(1)} %fusion.56, f32[]{:T(128)} %constant.11.clone.1, bf16[4096,256]{1,0:T(8,128)(2,1)S(1)} %gather_fusion, pred[4096]{0:T(1024)(128)(4,1)S(1)} %compare_and_fusion), kind=kCustom, calls=%fused_computation.41 | custom fusion | flops 4194304 | bytes 2380288 | tf_op jit(solution)/shard_map/scatter-add | solution.py:48
  424.9 70.0 %all-reduce.15.cloned.1.call-done = f32[256,256]{1,0:T(8,128)} async-done(((f32[256,256]{1,0:T(8,128)}), f32[256,256]{1,0:T(8,128)}) %all-reduce.15.cloned.1.call-update) | async-done | bytes 262160 | tf_op jit(solution)/shard_map/psum | solution.py:56
  494.9 1.4 multiply_reduce_fusion.10
  496.3 0.2 multiply_reduce_fusion.9
  496.5 0.8 broadcast_multiply_fusion
  497.4 16.1 %gather_fusion.4 = f32[4096,256]{1,0:T(8,128)} fusion(f32[256,256]{1,0:T(8,128)S(1)} %get-tuple-element.20, s32[4096]{0:T(1024)S(1)} %broadcast_clamp_fusion), kind=kCustom, calls=%fused_computation.4 | custom fusion | bytes 8404992 | tf_op jit(solution)/shard_map/gather | solution.py:47
  513.4 2.9 fusion.7
  516.4 26.1 %scatter_custom_fusion.4 = f32[256,256]{1,0:T(8,128)} fusion(s32[4096]{0:T(1024)} %bitcast.59, f32[4096]{0:T(1024)S(1)} %fusion.55, f32[]{:T(128)} %constant.11.clone.1, bf16[4096,256]{1,0:T(8,128)(2,1)S(1)} %gather_fusion, pred[4096]{0:T(1024)(128)(4,1)S(1)} %compare_and_fusion), kind=kCustom, calls=%fused_computation.43 | custom fusion | flops 4194304 | bytes 2380288 | tf_op jit(solution)/shard_map/scatter-add | solution.py:48
  542.6 69.9 %all-reduce.17.cloned.1.call-done = f32[256,256]{1,0:T(8,128)} async-done(((f32[256,256]{1,0:T(8,128)}), f32[256,256]{1,0:T(8,128)}) %all-reduce.17.cloned.1.call-update) | async-done | bytes 262160 | tf_op jit(solution)/shard_map/psum | solution.py:56
  612.5 1.4 multiply_reduce_fusion.8
  613.9 0.2 multiply_reduce_fusion.7
  614.3 16.1 %gather_fusion.5 = f32[4096,256]{1,0:T(8,128)} fusion(f32[256,256]{1,0:T(8,128)S(1)} %multiply_add_fusion.3, s32[4096]{0:T(1024)S(1)} %broadcast_clamp_fusion), kind=kCustom, calls=%fused_computation.5 | custom fusion | bytes 8404992 | tf_op jit(solution)/shard_map/gather | solution.py:47
  630.3 2.9 fusion.9
  633.3 35.0 %scatter_custom_fusion.5 = f32[256,256]{1,0:T(8,128)} fusion(s32[4096]{0:T(1024)} %bitcast.60, f32[4096]{0:T(1024)S(1)} %fusion.54, f32[]{:T(128)} %constant.11.clone.1, bf16[4096,256]{1,0:T(8,128)(2,1)S(1)} %gather_fusion, pred[4096]{0:T(1024)(128)(4,1)S(1)} %compare_and_fusion), kind=kCustom, calls=%fused_computation.45 | custom fusion | flops 4194304 | bytes 2380288 | tf_op jit(solution)/shard_map/scatter-add | solution.py:48
  668.4 70.0 %all-reduce.19.cloned.1.call-done = f32[256,256]{1,0:T(8,128)} async-done(((f32[256,256]{1,0:T(8,128)}), f32[256,256]{1,0:T(8,128)}) %all-reduce.19.cloned.1.call-update) | async-done | bytes 262160 | tf_op jit(solution)/shard_map/psum | solution.py:56
  738.4 1.4 multiply_reduce_fusion.6
  739.8 0.2 multiply_reduce_fusion.5
  740.1 16.1 %gather_fusion.6 = f32[4096,256]{1,0:T(8,128)} fusion(f32[256,256]{1,0:T(8,128)S(1)} %multiply_add_fusion.2, s32[4096]{0:T(1024)S(1)} %broadcast_clamp_fusion), kind=kCustom, calls=%fused_computation.6 | custom fusion | bytes 8404992 | tf_op jit(solution)/shard_map/gather | solution.py:47
  756.2 2.9 fusion.11
  759.2 26.1 %scatter_custom_fusion.6 = f32[256,256]{1,0:T(8,128)} fusion(s32[4096]{0:T(1024)} %bitcast.61, f32[4096]{0:T(1024)S(1)} %fusion.53, f32[]{:T(128)} %constant.11.clone.1, bf16[4096,256]{1,0:T(8,128)(2,1)S(1)} %gather_fusion, pred[4096]{0:T(1024)(128)(4,1)S(1)} %compare_and_fusion), kind=kCustom, calls=%fused_computation.47 | custom fusion | flops 4194304 | bytes 2380288 | tf_op jit(solution)/shard_map/scatter-add | solution.py:48
  785.3 70.0 %all-reduce.21.cloned.1.call-done = f32[256,256]{1,0:T(8,128)} async-done(((f32[256,256]{1,0:T(8,128)}), f32[256,256]{1,0:T(8,128)}) %all-reduce.21.cloned.1.call-update) | async-done | bytes 262160 | tf_op jit(solution)/shard_map/psum | solution.py:56
  855.3 1.4 multiply_reduce_fusion.4
  856.7 0.2 multiply_reduce_fusion.3
  857.0 0.7 copy-done.2
  857.8 16.1 %gather_fusion.7 = f32[4096,256]{1,0:T(8,128)} fusion(f32[256,256]{1,0:T(8,128)S(1)} %multiply_add_fusion.1, s32[4096]{0:T(1024)S(1)} %broadcast_clamp_fusion), kind=kCustom, calls=%fused_computation.7 | custom fusion | bytes 8404992 | tf_op jit(solution)/shard_map/gather | solution.py:47
  873.8 2.9 fusion.13
  876.8 26.1 %scatter_custom_fusion.7 = f32[256,256]{1,0:T(8,128)} fusion(s32[4096]{0:T(1024)} %bitcast.62, f32[4096]{0:T(1024)S(1)} %fusion.52, f32[]{:T(128)} %constant.11.clone.1, bf16[4096,256]{1,0:T(8,128)(2,1)S(1)} %gather_fusion, pred[4096]{0:T(1024)(128)(4,1)S(1)} %compare_and_fusion), kind=kCustom, calls=%fused_computation.49 | custom fusion | flops 4194304 | bytes 2380288 | tf_op jit(solution)/shard_map/scatter-add | solution.py:48
  903.0 70.0 %all-reduce.23.cloned.1.call-done = f32[256,256]{1,0:T(8,128)} async-done(((f32[256,256]{1,0:T(8,128)}), f32[256,256]{1,0:T(8,128)}) %all-reduce.23.cloned.1.call-update) | async-done | bytes 262160 | tf_op jit(solution)/shard_map/psum | solution.py:56
  973.0 1.4 multiply_reduce_fusion.2
  974.4 1.1 multiply_reduce_fusion.1
  975.6 0.7 copy-done.4
  976.4 16.1 %gather_fusion.8 = f32[4096,256]{1,0:T(8,128)} fusion(f32[256,256]{1,0:T(8,128)S(1)} %multiply_add_fusion, s32[4096]{0:T(1024)S(1)} %broadcast_clamp_fusion), kind=kCustom, calls=%fused_computation.8 | custom fusion | bytes 8404992 | tf_op jit(solution)/shard_map/gather | solution.py:47
  992.5 2.9 fusion.15
  995.4 26.1 %scatter_custom_fusion.8 = f32[256,256]{1,0:T(8,128)} fusion(s32[4096]{0:T(1024)} %bitcast.63, f32[4096]{0:T(1024)S(1)} %fusion.51, f32[]{:T(128)} %constant.11.clone.1, bf16[4096,256]{1,0:T(8,128)(2,1)S(1)} %gather_fusion, pred[4096]{0:T(1024)(128)(4,1)S(1)} %compare_and_fusion), kind=kCustom, calls=%fused_computation.51 | custom fusion | flops 4194304 | bytes 2380288 | tf_op jit(solution)/shard_map/scatter-add | solution.py:48
  1021.9 69.7 %all-reduce.25.cloned.1.call-done = f32[256,256]{1,0:T(8,128)} async-done(((f32[256,256]{1,0:T(8,128)}), f32[256,256]{1,0:T(8,128)}) %all-reduce.25.cloned.1.call-update) | async-done | bytes 262160 | tf_op jit(solution)/shard_map/psum | solution.py:56
  1091.6 1.5 multiply_reduce_fusion
  1093.2 1.5 fusion.43
  (60 shorter events, 1.5 us)
Async XLA Ops:
  7.2 25.5 %all-gather.3.cloned.1.call-start = ((), (), s32[]{:S(2)}) async-start(), calls=%async_computation.8 | async-start | bytes 2621440 | tf_op jit(solution)/shard_map/all_gather | solution.py:32
  7.9 134.3 %all-reduce.11.cloned.1.call-start = ((), (), s32[]{:S(2)}) async-start(), calls=%async_computation | async-start | bytes 524288 | tf_op jit(solution)/shard_map/psum | solution.py:53
  73.7 186.9 %all-reduce.27.cloned.1.call-start = ((), (), s32[]{:S(2)}) async-start(), calls=%async_computation.9 | async-start | bytes 1048576 | tf_op jit(solution)/shard_map/psum | solution.py:56
  159.2 3.0 copy-start.3
  159.2 101.4 %copy-start = (f32[256,256]{1,0:T(8,128)S(1)}, f32[256,256]{1,0:T(8,128)}, u32[]{:S(2)}) copy-start(f32[256,256]{1,0:T(8,128)} %all-reduce.11.cloned.1.call-done) | copy-start | bytes 786436
  188.4 188.9 %all-reduce.13.cloned.1.call-start = ((), (), s32[]{:S(2)}) async-start(), calls=%async_computation.1 | async-start | bytes 524288 | tf_op jit(solution)/shard_map/psum | solution.py:56
  278.6 98.7 %copy-start.1 = (f32[256,256]{1,0:T(8,128)S(1)}, f32[256,256]{1,0:T(8,128)}, u32[]{:S(2)}) copy-start(f32[256,256]{1,0:T(8,128)} %get-tuple-element.5) | copy-start | bytes 786436
  307.7 187.2 %all-reduce.15.cloned.1.call-start = ((), (), s32[]{:S(2)}) async-start(), calls=%async_computation.2 | async-start | bytes 524288 | tf_op jit(solution)/shard_map/psum | solution.py:56
  424.9 187.7 %all-reduce.17.cloned.1.call-start = ((), (), s32[]{:S(2)}) async-start(), calls=%async_computation.3 | async-start | bytes 524288 | tf_op jit(solution)/shard_map/psum | solution.py:56
  542.5 195.8 %all-reduce.19.cloned.1.call-start = ((), (), s32[]{:S(2)}) async-start(), calls=%async_computation.4 | async-start | bytes 524288 | tf_op jit(solution)/shard_map/psum | solution.py:56
  668.3 187.0 %all-reduce.21.cloned.1.call-start = ((), (), s32[]{:S(2)}) async-start(), calls=%async_computation.5 | async-start | bytes 524288 | tf_op jit(solution)/shard_map/psum | solution.py:56
  785.3 187.7 %all-reduce.23.cloned.1.call-start = ((), (), s32[]{:S(2)}) async-start(), calls=%async_computation.6 | async-start | bytes 524288 | tf_op jit(solution)/shard_map/psum | solution.py:56
  856.9 0.7 copy-start.2
  902.9 188.6 %all-reduce.25.cloned.1.call-start = ((), (), s32[]{:S(2)}) async-start(), calls=%async_computation.7 | async-start | bytes 524288 | tf_op jit(solution)/shard_map/psum | solution.py:56
  975.5 0.7 copy-start.4
Sparse Core Ops, SparseCore 0:
  9.6 23.0 all-gather.2
  73.8 68.3 all-reduce.10
  188.5 72.0 all-reduce.26
  307.8 69.4 all-reduce.12
  425.0 69.8 all-reduce.14
  542.7 69.8 all-reduce.16
  668.5 69.8 all-reduce.18
  785.4 69.8 all-reduce.20
  903.1 69.8 all-reduce.22
  1021.7 69.8 all-reduce.24
where the time goes:
time: 1110 us; the launch traced here: 1100 us
  waiting for transfers between devices  648 us (58%)
  other arithmetic  277 us (25%)
  local copies, waits for them, and re-layouts  146 us (13%)
  between operations  15.3 us (1%)
  matrix products  15.2 us (1%)
    psum x8, waiting for transfers between devices, image_every(): summed = lax.psum(local_terms(direction), 'ublk')  561 us
    scatter-add x8, other arithmetic, local_terms(): jax.ops.segment_sum(along[:, None] * rows, items, num_segments=column_items)  218 us
    gather x8, local copies, waits for them, and re-layouts, local_terms(): along = jnp.sum(rows * whole_dir[items], axis=1) * weight  130 us
    psum x1, waiting for transfers between devices, body(): rhs = lax.psum(rhs_terms, 'ublk')  64.8 us
    scatter-add x1, other arithmetic, body(): jax.ops.segment_sum(confid[:, None] * rows, items, num_segments=column_it...  26.1 us
    reduce_sum x8, other arithmetic, local_terms(): along = jnp.sum(rows * whole_dir[items], axis=1) * weight  23.6 us
  transfers between devices with their start and end apart: 10, of which 10 were waited for; matrix products, arithmetic and copies ran while one was open for 1% of the time, Pallas kernels for 0%

commit v1 on v0

--- a/solution.py
+++ b/solution.py
@@ -1,14 +1,21 @@
+import functools
+
 import jax
 import jax.numpy as jnp
 from jax import lax
+from jax.experimental import pallas as pl
+from jax.experimental.pallas import tpu as pltpu
 from jax.sharding import PartitionSpec as P
 
 ITERS = 8
 ITEM_DEV = 32
 
-
 REG = 1.0
 EPS = 1e-06
+
+LANES = 128
+STEP = 1024
+TABLE_BYTES = 1 << 25
 
 
 def conjugate(rhs, image_of):
@@ -27,7 +34,7 @@
     return (solution, resid)
 
 
-def body(user_factors, tile_users, tile_items, tile_weight, live_count):
+def reduced_body(user_factors, tile_users, tile_items, tile_weight, live_count):
     shard = user_factors[0]
     block = lax.all_gather(shard, "salt", axis=0, tiled=True)
     contract = (((0,), (0,)), ((), ()))
@@ -63,7 +70,184 @@
     return (solution[None], resid[None])
 
 
+def two_parts(value):
+    high = value.astype(jnp.bfloat16)
+    low = (value - high.astype(jnp.float32)).astype(jnp.bfloat16)
+    return jnp.concatenate([high, low], axis=0)
+
+
+def pick_rows(block, lo, hi, tile, first_ref, last_ref, keys_ref, weight_ref, table, rows, item_s, weight_s, count, total):
+    lane = lax.broadcasted_iota(jnp.int32, (LANES, LANES), 1)
+
+    def group(j, carry):
+        low = jnp.maximum(first_ref[block, j], lo)
+        high = jnp.minimum(last_ref[block, j], hi - 1)
+
+        @pl.when(low <= high)
+        def _():
+            at = count[0]
+            key = keys_ref[0, pl.ds(j, 1), :]
+            mine = (key >= lo) & (key < hi)
+            place = key - lo
+            user = jnp.where(mine, place // ITEM_DEV, -1)
+            item_s[pl.ds(at, 1), :] = jnp.where(mine, place % ITEM_DEV, -1)
+            weight_s[pl.ds(at, 1), :] = jnp.where(mine, weight_ref[0, pl.ds(j, 1), :], 0.0)
+            down = jnp.transpose(jnp.broadcast_to(user.astype(jnp.float32), (LANES, LANES))).astype(jnp.int32)
+            total[...] = jnp.zeros_like(total)
+
+            def part(t, inner):
+                start = pl.multiple_of(t * tile, tile)
+                ahead = down - start
+                hot = jnp.concatenate(
+                    [(ahead == lane + LANES * q).astype(jnp.bfloat16) for q in range(tile // LANES)], axis=1
+                )
+                total[...] += jnp.dot(hot, table[pl.ds(start, tile), :], preferred_element_type=jnp.float32)
+                return inner
+
+            lax.fori_loop((low - lo) // (ITEM_DEV * tile), (high - lo) // (ITEM_DEV * tile) + 1, part, 0)
+            rows[pl.ds(pl.multiple_of(at * LANES, LANES), LANES), :] = total[...].astype(rows.dtype)
+            count[0] = at + 1
+
+        return carry
+
+    lax.fori_loop(0, first_ref.shape[1], group, 0)
+
+
+def solve_items(rows, item_s, weight_s, count, gram, solution_ref, resid_ref):
+    groups = STEP // LANES
+    filled = count[0]
+    steps = (filled + groups - 1) // groups
+    for extra in range(groups - 1):
+        at = filled + extra
+
+        @pl.when(at < steps * groups)
+        def _():
+            rows[pl.ds(pl.multiple_of(at * LANES, LANES), LANES), :] = jnp.zeros((LANES, rows.shape[1]), rows.dtype)
+            item_s[pl.ds(at, 1), :] = jnp.full((1, LANES), -1, jnp.int32)
+            weight_s[pl.ds(at, 1), :] = jnp.zeros((1, LANES), jnp.float32)
+
+    own = lax.broadcasted_iota(jnp.int32, (ITEM_DEV, STEP), 0)
+
+    def along(ref, step):
+        return jnp.concatenate([ref[pl.ds(step * groups + g, 1), :] for g in range(groups)], axis=1)
+
+    def held(step):
+        return rows[pl.ds(pl.multiple_of(step * STEP, STEP), STEP), :]
+
+    def halves(pair):
+        return pair[:ITEM_DEV] + pair[ITEM_DEV:]
+
+    start = jnp.zeros((2 * ITEM_DEV, rows.shape[1]), jnp.float32)
+
+    def rhs_step(step, acc):
+        scaled = jnp.where(along(item_s, step) == own, 1.0 + along(weight_s, step), 0.0)
+        return acc + jnp.dot(two_parts(scaled), held(step), preferred_element_type=jnp.float32)
+
+    rhs = halves(lax.fori_loop(0, steps, rhs_step, start))
+
+    def image_of(direction):
+        parts = two_parts(direction)
+
+        def step_of(step, acc):
+            here = held(step)
+            dots = lax.dot_general(parts, here, (((1,), (1,)), ((), ())), preferred_element_type=jnp.float32)
+            scaled = jnp.where(along(item_s, step) == own, halves(dots) * along(weight_s, step), 0.0)
+            return acc + jnp.dot(two_parts(scaled), here, preferred_element_type=jnp.float32)
+
+        local = halves(lax.fori_loop(0, steps, step_of, start))
+        return local + jnp.dot(direction, gram[...], precision=lax.Precision.HIGHEST) + REG * direction
+
+    def iterate(_, state):
+        solution, resid, direction, norm_now = state
+        image = image_of(direction)
+        alpha = norm_now / (jnp.sum(direction * image, axis=1, keepdims=True) + EPS)
+        solution = solution + alpha * direction
+        resid = resid - alpha * image
+        norm_next = jnp.sum(resid * resid, axis=1, keepdims=True)
+        direction = resid + (norm_next / (norm_now + EPS)) * direction
+        return (solution, resid, direction, norm_next)
+
+    state = (jnp.zeros_like(rhs), rhs, rhs, jnp.sum(rhs * rhs, axis=1, keepdims=True))
+    solution, resid, _, _ = lax.fori_loop(0, ITERS, iterate, state)
+    solution_ref[...] = solution
+    resid_ref[...] = resid
+
+
+def solve_kernel(
+    tile, first_ref, last_ref, lo_ref, keys_ref, weight_ref, table_ref, solution_ref, resid_ref, rows, item_s, weight_s, gram, total, count
+):
+    block = pl.program_id(0)
+
+    @pl.when(block == 0)
+    def _():
+        count[0] = 0
+        gram[...] = jnp.zeros_like(gram)
+
+    lo = lo_ref[0]
+    hi = lo + table_ref.shape[0] * ITEM_DEV
+    gram[...] += lax.dot_general(
+        table_ref[...], table_ref[...], (((0,), (0,)), ((), ())), preferred_element_type=jnp.float32
+    )
+    pick_rows(block, lo, hi, tile, first_ref, last_ref, keys_ref, weight_ref, table_ref, rows, item_s, weight_s, count, total)
+
+    @pl.when(block == pl.num_programs(0) - 1)
+    def _():
+        solve_items(rows, item_s, weight_s, count, gram, solution_ref, resid_ref)
+
+
+def gathered_body(user_factors, tile_users, tile_items, tile_weight, live_count):
+    shard = user_factors[0]
+    blocks = lax.axis_size("ublk")
+    tile, rank = shard.shape
+    block_users = tile * lax.axis_size("salt")
+    slots = tile_users.shape[2]
+    groups = slots // LANES
+    live = jnp.arange(slots, dtype=jnp.int32) < live_count[0, 0]
+    items = tile_items[0, 0]
+    key = ((items // ITEM_DEV) * block_users + tile_users[0, 0]) * ITEM_DEV + items % ITEM_DEV
+    key = jnp.where(live, key, blocks * block_users * ITEM_DEV)
+    key, weight = lax.sort((key, tile_weight[0, 0]), num_keys=1, is_stable=False)
+    meta = lax.all_gather(jnp.stack([key.astype(jnp.float32), weight]), "ublk", axis=0)
+    keys = meta[:, 0].astype(jnp.int32).reshape(blocks, groups, LANES)
+    weights = meta[:, 1].reshape(blocks, groups, LANES)
+    lo = (lax.axis_index("ublk") * (block_users * ITEM_DEV)).astype(jnp.int32).reshape(1)
+    table = lax.all_gather(shard, ("ublk", "salt"), axis=0, tiled=True)
+    smem = pl.BlockSpec(memory_space=pltpu.SMEM)
+    out = jax.ShapeDtypeStruct((ITEM_DEV, rank), jnp.float32)
+    whole = pl.BlockSpec((ITEM_DEV, rank), lambda b: (0, 0))
+    capacity = blocks * slots + STEP
+    solution, resid = pl.pallas_call(
+        functools.partial(solve_kernel, tile),
+        grid=(blocks,),
+        in_specs=[
+            smem,
+            smem,
+            smem,
+            pl.BlockSpec((1, groups, LANES), lambda b: (b, 0, 0)),
+            pl.BlockSpec((1, groups, LANES), lambda b: (b, 0, 0)),
+            pl.BlockSpec((block_users, rank), lambda b: (b, 0)),
+        ],
+        out_specs=(whole, whole),
+        out_shape=(out, out),
+        scratch_shapes=[
+            pltpu.VMEM((capacity, rank), jnp.bfloat16),
+            pltpu.VMEM((capacity // LANES, LANES), jnp.int32),
+            pltpu.VMEM((capacity // LANES, LANES), jnp.float32),
+            pltpu.VMEM((rank, rank), jnp.float32),
+            pltpu.VMEM((LANES, rank), jnp.float32),
+            pltpu.SMEM((1,), jnp.int32),
+        ],
+        compiler_params=pltpu.CompilerParams(vmem_limit_bytes=40 << 20),
+    )(keys[:, :, 0], keys[:, :, LANES - 1], lo, keys, weights, table)
+    return (solution[None], resid[None])
+
+
 def solution(mesh):
+    def body(user_factors, *tiles):
+        table_bytes = user_factors.size * mesh.size * user_factors.dtype.itemsize
+        chosen = gathered_body if table_bytes <= TABLE_BYTES else reduced_body
+        return chosen(user_factors, *tiles)
+
     return jax.shard_map(
         body,
         mesh=mesh,

time: 1110 us -> 218 us (0.20)
  waiting for transfers between devices: 648 us -> 88 us
  other arithmetic: 277 us -> 6.71 us
  local copies, waits for them, and re-layouts: 146 us -> 0.43 us
  Pallas kernels: 0 us -> 82.1 us
  blocking collectives: 0 us -> 23.7 us
  matrix products: 15.2 us -> 0 us
    psum x9 -> x0, waiting for transfers between devices: 626 us -> none  [the longest x8 561 us: image_every(): summed = lax.psum(local_terms(direction), 'ublk')]
    scatter-add x9 -> x0, other arithmetic: 244 us -> none  [the longest x8 218 us: local_terms(): jax.ops.segment_sum(along[:, None] * rows, items, num_segments=column_items)]
    gather x9 -> x0, local copies, waits for them, and re-layouts: 144 us -> none  [the longest x8 130 us: local_terms(): along = jnp.sum(rows * whole_dir[items], axis=1) * weight]
    pallas_call x0 -> x1, Pallas kernels: none -> 82.1 us  [gathered_body(): pl.pallas_call(functools.partial(solve_kernel, tile), grid=(blocks,), in_...]
    all_gather x1, waiting for transfers between devices: 21.1 us -> 87.3 us  [gathered_body(): table = lax.all_gather(shard, ('ublk', 'salt'), axis=0, tiled=True)]
    reduce_sum x15 -> x0, other arithmetic: 26.6 us -> none  [the longest x8 23.6 us: local_terms(): along = jnp.sum(rows * whole_dir[items], axis=1) * weight]
    all_gather x0 -> x1, blocking collectives: none -> 23.7 us  [gathered_body(): lax.all_gather(jnp.stack([key.astype(jnp.float32), weight]), 'ublk', axis=0)]
    dot_general x9 -> x0, matrix products: 15.2 us -> none  [the longest x8 11.5 us: finish(): jnp.dot(direction, gram, precision=lax.Precision.HIGHEST)]
  transfers between devices with their start and end apart: 10 -> 1, of which waited for: 10 -> 1; matrix products, arithmetic and copies ran while one was open for 1% -> 3% of each run, Pallas kernels for 0% -> 0%
where the time goes in v1:
time: 218 us; the launch traced here: 216 us
  waiting for transfers between devices  88 us (40%)
  Pallas kernels  82.1 us (38%)
  blocking collectives  23.7 us (11%)
  between operations  14.7 us (7%)
  other arithmetic  6.71 us (3%)
    all_gather x1, waiting for transfers between devices, gathered_body(): table = lax.all_gather(shard, ('ublk', 'salt'), axis=0, tiled=True)  87.3 us
    pallas_call x1, Pallas kernels, gathered_body(): pl.pallas_call(functools.partial(solve_kernel, tile), grid=(blocks,), in_...  82.1 us
    all_gather x1, blocking collectives, gathered_body(): lax.all_gather(jnp.stack([key.astype(jnp.float32), weight]), 'ublk', axis=0)  23.7 us
    sort x1, other arithmetic, gathered_body(): lax.sort((key, tile_weight[0, 0]), num_keys=1, is_stable=False)  5.67 us
  transfers between devices with their start and end apart: 1, of which 1 were waited for; matrix products, arithmetic and copies ran while one was open for 3% of the time, Pallas kernels for 0%

profile of v1, /device:TPU:23, one launch (start us, length us, event | category | flops | bytes accessed | tf_op | source)
XLA Modules:
  0.0 215.8 jit_solution(1494247156138423955)
XLA Ops:
  7.2 0.0 all-gather.5.cloned.1.call-start
  7.2 0.7 all-gather.5.cloned.1.call-update
  8.5 0.8 fusion.4
  9.3 5.7 %sort.15 = (s32[4096]{0:T(1024)S(1)}, f32[4096]{0:T(1024)S(1)}) sort(s32[4096]{0:T(1024)S(1)} %fusion.4, f32[4096]{0:T(1024)} %bitcast.22), dimensions={0}, to_apply=%region_0.1 | sort | flops 49152 | bytes 65536 | tf_op jit(solution)/shard_map/sort | solution.py:209
  15.0 23.7 %all-gather.2 = f32[8,2,4096]{2,1,0:T(2,128)S(1)} all-gather(f32[1,2,4096]{2,1,0:T(2,128)S(1)} %maximum_bitcast_fusion), channel_id=2, replica_groups=mesh['ublk'=8,'salt'=4] {'ublk'}, dimensions={0}, use_global_device_ids=true | all-gather | bytes 294912 | tf_op jit(solution)/shard_map/all_gather | solution.py:210
  38.8 0.2 fusion.9
  39.0 0.4 slice_reduce_fusion
  39.4 87.3 %all-gather.5.cloned.1.call-done = bf16[1,32768,256]{2,1,0:T(8,128)(2,1)} async-done(((bf16[1,1024,256]{2,1,0:T(8,128)(2,1)}), bf16[1,32768,256]{2,1,0:T(8,128)(2,1)}) %all-gather.5.cloned.1.call-update) | async-done | bytes 16777232 | tf_op jit(solution)/shard_map/all_gather | solution.py:214
  126.8 82.1 %shard_map.68 = (f32[32,256]{1,0:T(8,128)}, f32[32,256]{1,0:T(8,128)}) custom-call(s32[8,32]{1,0:T(8,128)S(1)} %get-tuple-element.11.first_ref, s32[8,32]{1,0:T(8,128)S(1)} %get-tuple-element.10.last_ref, s32[1]{0:T(128)} %bitcast.8.lo_ref, s32[8,32,128]{2,1,0:T(8,128)S(1)} %bitcast.16, f32[8,32,128]{2,1,0:T(8,128)S(1)} %bitcast.17, bf16[32768,256]{1,0:T(8,128)(2,1)} %bitcast.18), custom_call_target="tpu_custom_call" | custom-call | tf_op jit(solution)/shard_map/pallas_call | solution.py:219
  (2 shorter events, 0.0 us)
Async XLA Ops:
  7.2 119.6 %all-gather.5.cloned.1.call-start = ((), (), s32[]{:S(2)}) async-start(), calls=%async_computation | async-start | bytes 17301504 | tf_op jit(solution)/shard_map/all_gather | solution.py:214
Sparse Core Ops, SparseCore 0:
  10.9 115.8 all-gather.4

commit v2 on v1

--- a/solution.py
+++ b/solution.py
@@ -1,5 +1,3 @@
-import functools
-
 import jax
 import jax.numpy as jnp
 from jax import lax
@@ -14,7 +12,8 @@
 EPS = 1e-06
 
 LANES = 128
-STEP = 1024
+STEP = 2048
+UNROLL = 64
 TABLE_BYTES = 1 << 25
 
 
@@ -76,41 +75,28 @@
     return jnp.concatenate([high, low], axis=0)
 
 
-def pick_rows(block, lo, hi, tile, first_ref, last_ref, keys_ref, weight_ref, table, rows, item_s, weight_s, count, total):
-    lane = lax.broadcasted_iota(jnp.int32, (LANES, LANES), 1)
-
-    def group(j, carry):
-        low = jnp.maximum(first_ref[block, j], lo)
-        high = jnp.minimum(last_ref[block, j], hi - 1)
-
-        @pl.when(low <= high)
-        def _():
-            at = count[0]
-            key = keys_ref[0, pl.ds(j, 1), :]
-            mine = (key >= lo) & (key < hi)
-            place = key - lo
-            user = jnp.where(mine, place // ITEM_DEV, -1)
-            item_s[pl.ds(at, 1), :] = jnp.where(mine, place % ITEM_DEV, -1)
-            weight_s[pl.ds(at, 1), :] = jnp.where(mine, weight_ref[0, pl.ds(j, 1), :], 0.0)
-            down = jnp.transpose(jnp.broadcast_to(user.astype(jnp.float32), (LANES, LANES))).astype(jnp.int32)
-            total[...] = jnp.zeros_like(total)
-
-            def part(t, inner):
-                start = pl.multiple_of(t * tile, tile)
-                ahead = down - start
-                hot = jnp.concatenate(
-                    [(ahead == lane + LANES * q).astype(jnp.bfloat16) for q in range(tile // LANES)], axis=1
-                )
-                total[...] += jnp.dot(hot, table[pl.ds(start, tile), :], preferred_element_type=jnp.float32)
-                return inner
-
-            lax.fori_loop((low - lo) // (ITEM_DEV * tile), (high - lo) // (ITEM_DEV * tile) + 1, part, 0)
-            rows[pl.ds(pl.multiple_of(at * LANES, LANES), LANES), :] = total[...].astype(rows.dtype)
-            count[0] = at + 1
-
-        return carry
-
-    lax.fori_loop(0, first_ref.shape[1], group, 0)
+def pick_rows(block, lo, hi, bounds_ref, users_ref, keys_ref, weight_ref, wide, rows, item_s, weight_s, count):
+    shift = ITEM_DEV.bit_length() - 1
+
+    def group(j, at):
+        key = keys_ref[0, pl.ds(j, 1), :]
+        mine = (key >= lo) & (key < hi)
+        item_s[pl.ds(at, 1), :] = jnp.where(mine, key & (ITEM_DEV - 1), -1)
+        weight_s[pl.ds(at, 1), :] = jnp.where(mine, weight_ref[0, pl.ds(j, 1), :], 0.0)
+
+        def some(i, carry):
+            base = pl.multiple_of(i * UNROLL, UNROLL)
+            taken = [wide[pl.ds(users_ref[0, 0, j * LANES + base + k], 1), :] for k in range(UNROLL)]
+            rows[pl.ds(pl.multiple_of(at * LANES + base, UNROLL), UNROLL), :] = jnp.concatenate(taken, axis=0).astype(rows.dtype)
+            return carry
+
+        lax.fori_loop(0, LANES // UNROLL, some, 0)
+        return at + 1
+
+    first = bounds_ref[block, 0]
+    last = bounds_ref[block, 1]
+    stop = jnp.where(last > first, (last + LANES - 1) // LANES, first // LANES)
+    count[0] = lax.fori_loop(first // LANES, stop, group, count[0])
 
 
 def solve_items(rows, item_s, weight_s, count, gram, solution_ref, resid_ref):
@@ -174,7 +160,7 @@
 
 
 def solve_kernel(
-    tile, first_ref, last_ref, lo_ref, keys_ref, weight_ref, table_ref, solution_ref, resid_ref, rows, item_s, weight_s, gram, total, count
+    bounds_ref, lo_ref, users_ref, keys_ref, weight_ref, table_ref, solution_ref, resid_ref, wide, rows, item_s, weight_s, gram, count
 ):
     block = pl.program_id(0)
 
@@ -188,7 +174,8 @@
     gram[...] += lax.dot_general(
         table_ref[...], table_ref[...], (((0,), (0,)), ((), ())), preferred_element_type=jnp.float32
     )
-    pick_rows(block, lo, hi, tile, first_ref, last_ref, keys_ref, weight_ref, table_ref, rows, item_s, weight_s, count, total)
+    wide[...] = table_ref[...].astype(jnp.float32)
+    pick_rows(block, lo, hi, bounds_ref, users_ref, keys_ref, weight_ref, wide, rows, item_s, weight_s, count)
 
     @pl.when(block == pl.num_programs(0) - 1)
     def _():
@@ -212,17 +199,21 @@
     weights = meta[:, 1].reshape(blocks, groups, LANES)
     lo = (lax.axis_index("ublk") * (block_users * ITEM_DEV)).astype(jnp.int32).reshape(1)
     table = lax.all_gather(shard, ("ublk", "salt"), axis=0, tiled=True)
+    hi = lo + block_users * ITEM_DEV
+    flat = keys.reshape(blocks, slots)
+    bounds = jnp.stack([jnp.sum((flat < lo).astype(jnp.int32), axis=1), jnp.sum((flat < hi).astype(jnp.int32), axis=1)], axis=1)
+    users = jnp.clip((flat - lo) // ITEM_DEV, 0, block_users - 1).reshape(blocks, 1, slots)
     smem = pl.BlockSpec(memory_space=pltpu.SMEM)
     out = jax.ShapeDtypeStruct((ITEM_DEV, rank), jnp.float32)
     whole = pl.BlockSpec((ITEM_DEV, rank), lambda b: (0, 0))
     capacity = blocks * slots + STEP
     solution, resid = pl.pallas_call(
-        functools.partial(solve_kernel, tile),
+        solve_kernel,
         grid=(blocks,),
         in_specs=[
             smem,
             smem,
-            smem,
+            pl.BlockSpec((1, 1, slots), lambda b: (b, 0, 0), memory_space=pltpu.SMEM),
             pl.BlockSpec((1, groups, LANES), lambda b: (b, 0, 0)),
             pl.BlockSpec((1, groups, LANES), lambda b: (b, 0, 0)),
             pl.BlockSpec((block_users, rank), lambda b: (b, 0)),
@@ -230,15 +221,15 @@
         out_specs=(whole, whole),
         out_shape=(out, out),
         scratch_shapes=[
+            pltpu.VMEM((block_users, rank), jnp.float32),
             pltpu.VMEM((capacity, rank), jnp.bfloat16),
             pltpu.VMEM((capacity // LANES, LANES), jnp.int32),
             pltpu.VMEM((capacity // LANES, LANES), jnp.float32),
             pltpu.VMEM((rank, rank), jnp.float32),
-            pltpu.VMEM((LANES, rank), jnp.float32),
             pltpu.SMEM((1,), jnp.int32),
         ],
         compiler_params=pltpu.CompilerParams(vmem_limit_bytes=40 << 20),
-    )(keys[:, :, 0], keys[:, :, LANES - 1], lo, keys, weights, table)
+    )(bounds, lo, users, keys, weights, table)
     return (solution[None], resid[None])
 
 

time: 218 us -> 188 us (0.86)
  the two profiles are of different devices: /device:TPU:23 before, /device:TPU:3 now
where the time goes in v2:
time: 188 us; the launch traced here: 189 us
  waiting for transfers between devices  86.9 us (46%)
  Pallas kernels  54 us (29%)
  blocking collectives  25.8 us (14%)
  between operations  14.7 us (8%)
  other arithmetic  7.94 us (4%)
    all_gather x1, waiting for transfers between devices, gathered_body(): table = lax.all_gather(shard, ('ublk', 'salt'), axis=0, tiled=True)  86.2 us
    pallas_call x1, Pallas kernels, gathered_body(): pl.pallas_call(solve_kernel, grid=(blocks,), in_specs=[smem, smem, pl.Blo...  54 us
    all_gather x1, blocking collectives, gathered_body(): lax.all_gather(jnp.stack([key.astype(jnp.float32), weight]), 'ublk', axis=0)  25.8 us
    sort x1, other arithmetic, gathered_body(): lax.sort((key, tile_weight[0, 0]), num_keys=1, is_stable=False)  5.67 us
  transfers between devices with their start and end apart: 1, of which 1 were waited for; matrix products, arithmetic and copies ran while one was open for 4% of the time, Pallas kernels for 0%

profile of v2, /device:TPU:3, one launch (start us, length us, event | category | flops | bytes accessed | tf_op | source)
XLA Modules:
  0.0 189.4 jit_solution(3209764089218511552)
XLA Ops:
  7.2 0.0 all-gather.5.cloned.1.call-start
  7.2 0.7 all-gather.5.cloned.1.call-update
  8.5 0.8 fusion.7
  9.3 5.7 %sort.15 = (s32[4096]{0:T(1024)S(1)}, f32[4096]{0:T(1024)S(1)}) sort(s32[4096]{0:T(1024)S(1)} %fusion.7, f32[4096]{0:T(1024)} %bitcast.24), dimensions={0}, to_apply=%region_0.1 | sort | flops 49152 | bytes 65536 | tf_op jit(solution)/shard_map/sort | solution.py:196
  15.0 25.8 %all-gather.2 = f32[8,2,4096]{2,1,0:T(2,128)S(1)} all-gather(f32[1,2,4096]{2,1,0:T(2,128)S(1)} %maximum_bitcast_fusion), channel_id=2, replica_groups=mesh['ublk'=8,'salt'=4] {'ublk'}, dimensions={0}, use_global_device_ids=true | all-gather | bytes 294912 | tf_op jit(solution)/shard_map/all_gather | solution.py:197
  40.8 1.2 fusion
  42.0 0.1 copy.9.bounds_ref
  42.1 0.2 fusion.12
  42.4 86.2 %all-gather.5.cloned.1.call-done = bf16[1,32768,256]{2,1,0:T(8,128)(2,1)} async-done(((bf16[1,1024,256]{2,1,0:T(8,128)(2,1)}), bf16[1,32768,256]{2,1,0:T(8,128)(2,1)}) %all-gather.5.cloned.1.call-update) | async-done | bytes 16777232 | tf_op jit(solution)/shard_map/all_gather | solution.py:201
  128.6 54.0 %shard_map.68 = (f32[32,256]{1,0:T(8,128)}, f32[32,256]{1,0:T(8,128)}) custom-call(s32[8,2]{1,0:T(8,128)S(1)} %copy.9.bounds_ref, s32[1]{0:T(128)} %bitcast.8.lo_ref, s32[8,1,4096]{2,1,0:T(1,128)S(1)} %get-tuple-element.14.users_ref, s32[8,32,128]{2,1,0:T(8,128)S(1)} %bitcast.19, f32[8,32,128]{2,1,0:T(8,128)S(1)} %bitcast.18, bf16[32768,256]{1,0:T(8,128)(2,1)} %bitcast.20), custom_call_target="tpu_custom_call" | custom-call | tf_op jit(solution)/shard_map/pallas_call | solution.py:210
  (3 shorter events, 0.0 us)
Async XLA Ops:
  7.2 121.4 %all-gather.5.cloned.1.call-start = ((), (), s32[]{:S(2)}) async-start(), calls=%async_computation | async-start | bytes 17301504 | tf_op jit(solution)/shard_map/all_gather | solution.py:201
Sparse Core Ops, SparseCore 0:
  10.9 117.6 all-gather.4
